TPU v7x, 32 devices: a whole 2x2x4 slice. The times are simulated.
32 devices in a mesh: grp: 2 (over y), blk: 4 (over z), col: 2 (over x), rep: 2 (over core).
Axes of the slice: x: 2, y: 2, z: 4, core: 2. Of those that a mesh axis runs over, the one named last changes fastest.
Arguments:
- coords: float32 [3, 131072], P(None, ('grp', 'blk')), parts along dimension 1, may hold values from 0 to 1
- observations: float32 [131072], P(('grp', 'blk')), parts along dimension 0, may hold values from -6 to 6
- nugget: float32 [131072], P(('grp', 'blk')), parts along dimension 0, may hold values from 0.1 to 1
- tile_pairs: int32 [2, 8192], P(None, ('grp', 'blk', 'col', 'rep')), parts along dimension 1, may hold values from 0 to 511, as said below
- tile_live: int32 [32], P(('grp', 'blk', 'col', 'rep')), parts along dimension 0, may hold values from 64 to 256, as said below
Outputs:
- solution_field: float32 [131072], P(('grp', 'blk')), parts along dimension 0
- residual: float32 [131072], P(('grp', 'blk')), parts along dimension 0
There are 2 independent parts, one for each index of `grp`. A program takes and returns all parts, laid end to end along the dimension named above; each array names one. Nothing has to cross between parts.
Inputs may be any that keep to these rules, and one draw needn't show every extreme that they name: `tile_pairs`: entries name point blocks. Every slot has its row block, or else its column block, among the 128 blocks of its own device's index of blk; most slots have the row block there. Call the slot's other block its column block when the row block is the device's own, else its row block. Of one device's slots, at most (259) // 4 have their other block among the blocks of any one index of blk, and on every device some index gets exactly that many. Slots at or beyond a device's live count are ignored. `tile_live`: some device has all 256 slots live.
All inputs are finite; a program needn't handle non-finite values.
Results may differ from a plain program's by a relative error of at most 0.0003.
Values sent between devices are 32-bit elements; how exact they have to be, the bound alone decides.
No kernel may reach another device: no remote copies, remote signals or barrier semaphores. Data moves between devices by JAX's collectives and lax.ppermute only.
A program may use at most 128 MiB of HBM per device.

v0:
```python
import jax
import jax.numpy as jnp
from jax import lax
from jax.sharding import PartitionSpec as P

BS = 128
ITERS = 3


support = 0.3


def pair_totals(residual, mapped):
    return lax.psum((jnp.sum(residual * residual), jnp.sum(residual * mapped)), "blk")


def build_tiles(grouped, first_ids, second_ids, weights, amplitude):
    first_points = jnp.take(grouped, first_ids, axis=1)
    second_points = jnp.take(grouped, second_ids, axis=1)
    offset = first_points[:, :, :, None] - second_points[:, :, None, :]
    scaled = jnp.sqrt(jnp.sum(offset * offset, axis=0)) / support
    remain = jnp.maximum(1.0 - scaled, 0.0)
    return amplitude * remain**4 * (4.0 * scaled + 1.0) * weights[:, None, None]


def local(coords, observations, nugget, tile_pairs, tile_live):
    all_coords = lax.all_gather(coords, "blk", axis=1, tiled=True)
    block_count = all_coords.shape[1] // BS
    slot_count = tile_pairs.shape[1]
    blk_count = lax.axis_size("blk")
    per_row = slot_count * lax.axis_size("col") * lax.axis_size("rep") * blk_count // block_count
    amplitude = 16.0 / (BS * per_row)
    grouped = all_coords.reshape(3, block_count, BS)
    rows_ids = tile_pairs[0]
    cols_ids = tile_pairs[1]
    alive_mask = (jnp.arange(slot_count) < tile_live[0]).astype(jnp.float32)
    highest = lax.Precision.HIGHEST
    block_ids = jnp.arange(block_count, dtype=jnp.int32)
    tiles = build_tiles(grouped, rows_ids, cols_ids, alive_mask, amplitude)
    row_onehot = (rows_ids[:, None] == block_ids[None, :]).astype(jnp.float32)
    col_onehot = (cols_ids[:, None] == block_ids[None, :]).astype(jnp.float32)

    def apply_off(whole):
        blocks = whole.reshape(block_count, BS)
        col_vecs = jnp.take(blocks, cols_ids, axis=0)
        row_vecs = jnp.take(blocks, rows_ids, axis=0)
        forward = jnp.einsum("sac,sc->sa", tiles, col_vecs, precision=highest)
        backward = jnp.einsum("sac,sa->sc", tiles, row_vecs, precision=highest)
        partial_value = jnp.einsum("sb,sa->ba", row_onehot, forward, precision=highest)
        partial_value = partial_value + jnp.einsum(
            "sb,sa->ba", col_onehot, backward, precision=highest
        )
        partial_value = partial_value.reshape(block_count * BS)
        joined = lax.psum(partial_value, ("col", "rep"))
        return lax.psum_scatter(joined, "blk", scatter_dimension=0, tiled=True)

    diagonal = nugget + apply_off(jnp.ones((block_count * BS,), jnp.float32))

    def mapped_of(vector_in):
        whole = lax.all_gather(vector_in, "blk", axis=0, tiled=True)
        return diagonal * vector_in + apply_off(whole)

    solution_field = jnp.zeros_like(observations)
    residual = observations
    mapped = mapped_of(residual)
    norm_now, product = pair_totals(residual, mapped)
    step_len = norm_now / product
    direction, along_vec = (residual, mapped)
    for sweep in range(ITERS):
        solution_field = solution_field + step_len * direction
        residual = residual - step_len * along_vec
        if sweep + 1 < ITERS:
            mapped = mapped_of(residual)
            norm_next, product = pair_totals(residual, mapped)
            beta_ratio = norm_next / norm_now
            step_len = norm_next / (product - beta_ratio * norm_next / step_len)
            direction = residual + beta_ratio * direction
            along_vec = mapped + beta_ratio * along_vec
            norm_now = norm_next
    return (solution_field, residual)


def solution(mesh):
    in_specs = (
        P(None, ("grp", "blk")),
        P(("grp", "blk")),
        P(("grp", "blk")),
        P(None, ("grp", "blk", "col", "rep")),
        P(("grp", "blk", "col", "rep")),
    )
    out_specs = (P(("grp", "blk")), P(("grp", "blk")))
    return jax.shard_map(local, mesh=mesh, in_specs=in_specs, out_specs=out_specs, check_vma=False)
```

profile of v0, /device:TPU:0, one launch (start us, length us, event | category | flops | bytes accessed | tf_op | source)
XLA Modules:
  0.0 567.7 jit_solution(2386943631072973725)
XLA Ops:
  7.2 0.8 fusion.16
  8.0 24.4 %all_gather.12 = f32[3,65536]{1,0:T(4,128)S(1)} all-gather(f32[3,16384]{1,0:T(4,128)} %param.9), channel_id=1, replica_groups=mesh['grp'=2,'blk'=4,'col'=2,'rep'=2] {'blk'}, dimensions={1}, use_global_device_ids=true | all-gather | bytes 983040 | tf_op jit(solution)/shard_map/all_gather | solution.py:27
  32.4 1.0 gather_fusion
  33.4 1.0 gather_fusion.1
  34.5 0.7 gather_fusion.2
  35.2 0.7 gather_fusion.3
  35.9 14.4 %all_gather.13 = f32[65536]{0:T(1024)S(1)} all-gather(f32[16384]{0:T(1024)} %param.10), channel_id=1, replica_groups=mesh['grp'=2,'blk'=4,'col'=2,'rep'=2] {'blk'}, dimensions={0}, use_global_device_ids=true | all-gather | bytes 327680 | tf_op jit(solution)/shard_map/all_gather | solution.py:60
  50.4 0.7 gather_fusion.4
  51.1 0.7 gather_fusion.5
  53.2 22.2 %multiply_reduce_fusion = f32[256,128,128]{2,1,0:T(8,128)} fusion(f32[3,256,128]{2,1,0:T(8,128)S(1)} %copy.12, f32[3,256,128]{2,1,0:T(8,128)S(1)} %copy.11), kind=kLoop, calls=%fused_computation.10 | loop fusion | flops 33554432 | bytes 17563648 | tf_op jit(solution)/shard_map/reduce_sum | solution.py:21
  75.4 12.1 %multiply_multiply_fusion = f32[256,128,128]{2,1,0:T(8,128)S(1)} fusion(f32[256,128,128]{2,1,0:T(8,128)} %multiply_reduce_fusion, f32[256]{0:T(256)S(1)} %compare_convert_fusion), kind=kLoop, calls=%fused_computation.11 | loop fusion | flops 41943040 | bytes 33555456 | tf_op jit(solution)/shard_map/mul | solution.py:23
  87.7 26.5 %fusion.17 = f32[256,1,128]{2,1,0:T(1,128)S(1)} fusion(f32[256,128,128]{2,1,0:T(8,128)S(1)} %multiply_multiply_fusion, f32[256,128,1]{1,2,0:T(1,128)S(1)} %bitcast.99), kind=kOutput, calls=%fused_computation.66 | convolution fusion | flops 50331648 | bytes 17039360 | tf_op jit(solution)/shard_map/sac,sc->sa/dot_general | solution.py:47
  115.0 15.0 %fusion.18 = f32[256,1,128]{2,1,0:T(1,128)S(1)} fusion(f32[256,128,128]{2,1,0:T(8,128)S(1)} %multiply_multiply_fusion, f32[256,128,1]{1,2,0:T(1,128)S(1)} %bitcast.100), kind=kOutput, calls=%fused_computation.67 | convolution fusion | flops 50331648 | bytes 17039360 | tf_op jit(solution)/shard_map/sac,sa->sc/dot_general | solution.py:48
  130.0 26.5 %fusion.19 = f32[256,1,128]{2,1,0:T(1,128)S(1)} fusion(f32[256,128,128]{2,1,0:T(8,128)S(1)} %multiply_multiply_fusion, f32[256,128,1]{1,2,0:T(1,128)S(1)} %bitcast.93), kind=kOutput, calls=%fused_computation.68 | convolution fusion | flops 50331648 | bytes 17039360 | tf_op jit(solution)/shard_map/sac,sc->sa/dot_general | solution.py:47
  157.2 14.7 %fusion.20 = f32[256,1,128]{2,1,0:T(1,128)S(1)} fusion(f32[256,128,128]{2,1,0:T(8,128)S(1)} %multiply_multiply_fusion, f32[256,128,1]{1,2,0:T(1,128)S(1)} %bitcast.95), kind=kOutput, calls=%fused_computation.69 | convolution fusion | flops 50331648 | bytes 17039360 | tf_op jit(solution)/shard_map/sac,sa->sc/dot_general | solution.py:48
  172.0 1.4 fusion.3
  173.4 1.4 fusion.2
  176.1 37.2 %all-reduce.26.cloned.1.call-done = (f32[65536]{0:T(1024)}, f32[65536]{0:T(1024)}) async-done(((f32[65536]{0:T(1024)}, f32[65536]{0:T(1024)}), (f32[65536]{0:T(1024)}, f32[65536]{0:T(1024)})) %all-reduce.26.cloned.1.call-update) | async-done | bytes 524304
  213.3 1.5 dynamic-slice.1
  214.8 1.5 dynamic-slice.3
  216.4 31.6 %all-reduce.24.cloned.1.call-done = (f32[16384]{0:T(1024)}, f32[16384]{0:T(1024)}) async-done(((f32[16384]{0:T(1024)}, f32[16384]{0:T(1024)}), (f32[16384]{0:T(1024)}, f32[16384]{0:T(1024)})) %all-reduce.24.cloned.1.call-update) | async-done | bytes 131088 | tf_op jit(solution)/shard_map/psum | solution.py:54
  247.9 1.5 multiply_reduce_fusion.5
  249.4 12.4 %all-reduce.7 = (f32[]{:T(128)}, f32[]{:T(128)}) all-reduce(f32[]{:T(128)} %get-tuple-element.9, f32[]{:T(128)} %get-tuple-element.8), channel_id=1, replica_groups=mesh['grp'=2,'blk'=4,'col'=2,'rep'=2] {'blk'}, use_global_device_ids=true, to_apply=%region_1.2 | all-reduce | flops 2 | bytes 16 | tf_op jit(solution)/shard_map/psum | solution.py:14
  263.2 0.9 multiply_subtract_fusion.2
  264.0 13.8 %all_gather.14 = f32[65536]{0:T(1024)S(1)} all-gather(f32[16384]{0:T(1024)S(1)} %multiply_subtract_fusion.2), channel_id=1, replica_groups=mesh['grp'=2,'blk'=4,'col'=2,'rep'=2] {'blk'}, dimensions={0}, use_global_device_ids=true | all-gather | bytes 327680 | tf_op jit(solution)/shard_map/all_gather | solution.py:60
  277.8 0.7 gather_fusion.7
  278.5 0.7 gather_fusion.6
  279.4 17.7 %fusion.22 = f32[256,1,128]{2,1,0:T(1,128)S(1)} fusion(f32[256,128,128]{2,1,0:T(8,128)} %copy-done, f32[256,128,1]{1,2,0:T(1,128)S(1)} %bitcast.107), kind=kOutput, calls=%fused_computation.71 | convolution fusion | flops 50331648 | bytes 17039360 | tf_op jit(solution)/shard_map/sac,sa->sc/dot_general | solution.py:48
  297.2 26.5 %fusion.21 = f32[256,1,128]{2,1,0:T(1,128)S(1)} fusion(f32[256,128,128]{2,1,0:T(8,128)S(1)} %copy-done.1, f32[256,128,1]{1,2,0:T(1,128)S(1)} %bitcast.108), kind=kOutput, calls=%fused_computation.70 | convolution fusion | flops 50331648 | bytes 17039360 | tf_op jit(solution)/shard_map/sac,sc->sa/dot_general | solution.py:47
  324.4 1.4 fusion.1
  325.9 32.9 %all-reduce.20.cloned.1.call-done = f32[65536]{0:T(1024)} async-done(((f32[65536]{0:T(1024)}), f32[65536]{0:T(1024)}) %all-reduce.20.cloned.1.call-update) | async-done | bytes 262160
  358.7 1.5 dynamic-slice.5
  360.3 32.0 %all-reduce.16.cloned.1.call-done = f32[16384]{0:T(1024)} async-done(((f32[16384]{0:T(1024)}), f32[16384]{0:T(1024)}) %all-reduce.16.cloned.1.call-update) | async-done | bytes 65552 | tf_op jit(solution)/shard_map/psum | solution.py:54
  392.3 1.5 multiply_reduce_fusion.3
  393.8 12.3 %all-reduce.6 = (f32[]{:T(128)}, f32[]{:T(128)}) all-reduce(f32[]{:T(128)} %get-tuple-element.7, f32[]{:T(128)} %get-tuple-element.6), channel_id=1, replica_groups=mesh['grp'=2,'blk'=4,'col'=2,'rep'=2] {'blk'}, use_global_device_ids=true, to_apply=%region_10.13 | all-reduce | flops 2 | bytes 16 | tf_op jit(solution)/shard_map/psum | solution.py:14
  410.7 0.9 multiply_subtract_fusion.1
  411.5 13.8 %all_gather.15 = f32[65536]{0:T(1024)S(1)} all-gather(f32[16384]{0:T(1024)S(1)} %multiply_subtract_fusion.1), channel_id=1, replica_groups=mesh['grp'=2,'blk'=4,'col'=2,'rep'=2] {'blk'}, dimensions={0}, use_global_device_ids=true | all-gather | bytes 327680 | tf_op jit(solution)/shard_map/all_gather | solution.py:60
  425.3 0.7 gather_fusion.9
  426.1 0.7 gather_fusion.8
  426.9 17.0 %fusion.24 = f32[256,1,128]{2,1,0:T(1,128)S(1)} fusion(f32[256,128,128]{2,1,0:T(8,128)} %copy-done, f32[256,128,1]{1,2,0:T(1,128)S(1)} %bitcast.106), kind=kOutput, calls=%fused_computation.73 | convolution fusion | flops 50331648 | bytes 17039360 | tf_op jit(solution)/shard_map/sac,sa->sc/dot_general | solution.py:48
  444.0 28.6 %fusion.23 = f32[256,1,128]{2,1,0:T(1,128)S(1)} fusion(f32[256,128,128]{2,1,0:T(8,128)} %copy-done, f32[256,128,1]{1,2,0:T(1,128)S(1)} %bitcast.105), kind=kOutput, calls=%fused_computation.72 | convolution fusion | flops 50331648 | bytes 17039360 | tf_op jit(solution)/shard_map/sac,sc->sa/dot_general | solution.py:47
  473.3 1.4 fusion
  474.8 32.9 %all-reduce.22.cloned.1.call-done = f32[65536]{0:T(1024)} async-done(((f32[65536]{0:T(1024)}), f32[65536]{0:T(1024)}) %all-reduce.22.cloned.1.call-update) | async-done | bytes 262160
  507.6 1.5 dynamic-slice.7
  509.1 32.1 %all-reduce.18.cloned.1.call-done = f32[16384]{0:T(1024)} async-done(((f32[16384]{0:T(1024)}), f32[16384]{0:T(1024)}) %all-reduce.18.cloned.1.call-update) | async-done | bytes 65552 | tf_op jit(solution)/shard_map/psum | solution.py:54
  541.2 1.5 multiply_reduce_fusion.1
  542.7 12.3 %all-reduce.5 = (f32[]{:T(128)}, f32[]{:T(128)}) all-reduce(f32[]{:T(128)} %get-tuple-element.5, f32[]{:T(128)} %get-tuple-element.4), channel_id=1, replica_groups=mesh['grp'=2,'blk'=4,'col'=2,'rep'=2] {'blk'}, use_global_device_ids=true, to_apply=%region_16.19 | all-reduce | flops 2 | bytes 16 | tf_op jit(solution)/shard_map/psum | solution.py:14
  558.9 1.5 multiply_subtract_fusion
  (49 shorter events, 5.2 us)
Async XLA Ops:
  7.2 206.2 %all-reduce.26.cloned.1.call-start = ((), (), s32[]{:S(2)}) async-start(), calls=%async_computation.5 | async-start | bytes 1048576
  87.6 69.7 %copy-start = (f32[256,128,128]{2,1,0:T(8,128)}, f32[256,128,128]{2,1,0:T(8,128)S(1)}, u32[]{:S(2)}) copy-start(f32[256,128,128]{2,1,0:T(8,128)S(1)} %multiply_multiply_fusion) | copy-start | bytes 50331652
  130.0 44.9 %copy-start.6 = (u32[32]{0:T(128)S(1)}, u32[32]{0:T(128)}, u32[]{:S(2)}) copy-start(u32[32]{0:T(128)} %constant.12) | copy-start | bytes 388
  130.0 117.9 %copy-start.2 = (f32[16384]{0:T(1024)S(1)}, f32[16384]{0:T(1024)}, u32[]{:S(2)}) copy-start(f32[16384]{0:T(1024)} %param.10) | copy-start | bytes 196612
  130.0 117.9 %copy-start.5 = (f32[16384]{0:T(1024)S(1)}, f32[16384]{0:T(1024)}, u32[]{:S(2)}) copy-start(f32[16384]{0:T(1024)} %param.11) | copy-start | bytes 196612
  174.8 73.1 %all-reduce.24.cloned.1.call-start = ((), (), s32[]{:S(2)}) async-start(), calls=%async_computation.4 | async-start | bytes 262144 | tf_op jit(solution)/shard_map/psum | solution.py:54
  216.3 142.4 %all-reduce.20.cloned.1.call-start = ((), (), s32[]{:S(2)}) async-start(), calls=%async_computation.2 | async-start | bytes 524288
  279.3 17.9 %copy-start.1 = (f32[256,128,128]{2,1,0:T(8,128)S(1)}, f32[256,128,128]{2,1,0:T(8,128)}, u32[]{:S(2)}) copy-start(f32[256,128,128]{2,1,0:T(8,128)} %copy-done) | copy-start | bytes 50331652
  279.4 131.3 %copy-start.3 = (f32[16384]{0:T(1024)S(1)}, f32[16384]{0:T(1024)}, u32[]{:S(2)}) copy-start(f32[16384]{0:T(1024)} %get-tuple-element.10) | copy-start | bytes 196612
  325.8 66.5 %all-reduce.16.cloned.1.call-start = ((), (), s32[]{:S(2)}) async-start(), calls=%async_computation | async-start | bytes 131072 | tf_op jit(solution)/shard_map/psum | solution.py:54
  360.2 147.4 %all-reduce.22.cloned.1.call-start = ((), (), s32[]{:S(2)}) async-start(), calls=%async_computation.3 | async-start | bytes 524288
  426.9 132.0 %copy-start.4 = (f32[16384]{0:T(1024)S(1)}, f32[16384]{0:T(1024)}, u32[]{:S(2)}) copy-start(f32[16384]{0:T(1024)} %all-reduce.16.cloned.1.call-done) | copy-start | bytes 196612
  474.7 66.5 %all-reduce.18.cloned.1.call-start = ((), (), s32[]{:S(2)}) async-start(), calls=%async_computation.1 | async-start | bytes 131072 | tf_op jit(solution)/shard_map/psum | solution.py:54
Sparse Core Ops, SparseCore 0:
  174.9 38.3 all-reduce.25
  216.4 31.4 all-reduce.23
  325.9 32.7 all-reduce.19
  361.5 30.7 all-reduce.15
  474.8 32.7 all-reduce.21
  510.4 30.7 all-reduce.17
where the time goes:
time: 578 us; the launch traced here: 568 us
  waiting for transfers between devices  199 us (34%)
  matrix products  181 us (31%)
  blocking collectives  103 us (18%)
  other arithmetic  43.4 us (8%)
  between operations  26 us (4%)
  local copies, waits for them, and re-layouts  15.2 us (3%)
    dot_general x4, matrix products, apply_off(): forward = jnp.einsum('sac,sc->sa', tiles, col_vecs, precision=highest)  108 us
    unnamed x9, waiting for transfers between devices  103 us
    psum x3, waiting for transfers between devices, apply_off(): joined = lax.psum(partial_value, ('col', 'rep'))  95.7 us
    dot_general x4, matrix products, apply_off(): backward = jnp.einsum('sac,sa->sc', tiles, row_vecs, precision=highest)  64.4 us
    all_gather x3, blocking collectives, mapped_of(): whole = lax.all_gather(vector_in, 'blk', axis=0, tiled=True)  42 us
    psum x3, blocking collectives, pair_totals(): lax.psum((jnp.sum(residual * residual), jnp.sum(residual * mapped)), 'blk')  37 us
    all_gather x1, blocking collectives, local(): all_coords = lax.all_gather(coords, 'blk', axis=1, tiled=True)  24.4 us
    reduce_sum x1, other arithmetic, build_tiles(): scaled = jnp.sqrt(jnp.sum(offset * offset, axis=0)) / support  22.2 us
  transfers between devices with their start and end apart: 6, of which 6 were waited for; matrix products, arithmetic and copies ran while one was open for 0% of the time, Pallas kernels for 0%

commit v1 on v0

v1 whole, which is shorter than its diff:
```python
import functools

import jax
import jax.numpy as jnp
from jax import lax
from jax.experimental import pallas as pl
from jax.experimental.pallas import tpu as pltpu
from jax.sharding import PartitionSpec as P

BS = 128
ITERS = 3
SUPPORT = 0.3
DEPTH = 48
UNROLL = 4
EVERY = ("blk", "col", "rep")
PLANE = ("col", "rep")
VMEM = pl.BlockSpec(memory_space=pltpu.VMEM)
SMEM = pl.BlockSpec(memory_space=pltpu.SMEM)
PARAMS = pltpu.CompilerParams(vmem_limit_bytes=48 * 1024 * 1024)
BF16 = jnp.bfloat16
F32 = jnp.float32


class Sizes:
    def __init__(self, points, slots):
        self.blks = lax.axis_size("blk")
        self.reps = lax.axis_size("rep")
        self.plane = lax.axis_size("col") * self.reps
        self.devs = self.blks * self.plane
        self.points = points
        self.slots = slots
        self.local_blocks = points // BS
        self.blocks = self.local_blocks * self.blks
        self.own = self.local_blocks // self.plane
        self.capacity = 2 * self.plane * slots
        per_row = slots * self.devs // self.blocks
        self.scale = 16.0 / (BS * per_row) / 256.0

    def me(self):
        return (lax.axis_index("blk") * lax.axis_size("col") + lax.axis_index("col")) * self.reps + lax.axis_index(
            "rep"
        )


def swap(x, axes, count, code):
    return lax.ppermute(x, axes, [(i, i ^ code) for i in range(count)])


def spread(x, sz):
    if sz.devs <= 16:
        return [x] + [swap(x, EVERY, sz.devs, s) for s in range(1, sz.devs)], [[s] for s in range(sz.devs)]
    column = jnp.concatenate([x] + [swap(x, "blk", sz.blks, s) for s in range(1, sz.blks)], axis=0)
    arrays = [column] + [swap(column, PLANE, sz.plane, s) for s in range(1, sz.plane)]
    return arrays, [[z * sz.plane + s for z in range(sz.blks)] for s in range(sz.plane)]


def assemble(refs, codes, me, rows, target):
    for ref, parts in zip(refs, codes):
        for k, code in enumerate(parts):
            start = pl.multiple_of(jnp.bitwise_xor(me, code) * rows, 8)
            target[pl.ds(start, rows), :] = ref[k * rows : (k + 1) * rows, :]


def split3(x):
    high = x.astype(BF16).astype(F32)
    rest = x - high
    middle = rest.astype(BF16).astype(F32)
    return high, middle, rest - middle


def lhs_kernel(sz, coords_ref, out_ref):
    quarter = lax.axis_index("col") * sz.reps + lax.axis_index("rep")
    unit = jnp.ones((1, BS), F32)
    for i in range(sz.own):
        start = pl.multiple_of((quarter * sz.own + i) * BS, BS)
        x = (coords_ref[:, pl.ds(start, BS)] - 0.5) * (4.0 / SUPPORT)
        norm = jnp.sum(x * x, axis=0, keepdims=True)
        h, m, l = split3(jnp.concatenate([x, unit, norm, jnp.zeros((3, BS), F32)], axis=0))
        feats = jnp.concatenate([h, h, m, m, h, l, jnp.zeros((BS - DEPTH, BS), F32)], axis=0)
        out_ref[i * BS : (i + 1) * BS, :] = feats.T.astype(BF16)
    out_ref[sz.own * BS :, :] = jnp.zeros((BS, BS), BF16)


def list_kernel(sz, codes, *refs):
    pieces = refs[: len(codes)]
    out_ref, count_ref, target, other, place, value = refs[len(codes) :]
    me = sz.me()
    lines = sz.slots // BS
    at = 0
    for ref, parts in zip(pieces, codes):
        for k in range(len(parts)):
            base = 2 * lines * k
            rows = ref[base : base + lines, :]
            cols = ref[base + lines : base + 2 * lines, :]
            target[at : at + lines, :] = rows
            other[at : at + lines, :] = cols
            target[at + lines : at + 2 * lines, :] = cols
            other[at + lines : at + 2 * lines, :] = rows
            at += 2 * lines
    local = target[...] - me * sz.own
    mine = jnp.logical_and(local >= 0, local < sz.own)
    flags = jnp.where(mine, 1.0, 0.0)
    a = lax.broadcasted_iota(jnp.int32, (BS, BS), 0)
    b = lax.broadcasted_iota(jnp.int32, (BS, BS), 1)
    before = jnp.dot(flags.astype(BF16), jnp.where(a < b, 1.0, 0.0).astype(BF16), preferred_element_type=F32)
    totals = jnp.broadcast_to(jnp.sum(flags, axis=1, keepdims=True), (at, BS))
    a = lax.broadcasted_iota(jnp.int32, (at, at), 0)
    b = lax.broadcasted_iota(jnp.int32, (at, at), 1)
    above = jnp.dot(jnp.where(b < a, 1.0, 0.0).astype(BF16), totals.astype(BF16), preferred_element_type=F32)
    place[...] = jnp.where(mine, above + before, -1.0)
    value[...] = (local + 256 * other[...]).astype(F32)
    count = jnp.sum(flags).astype(jnp.int32)
    count_ref[0] = count
    sub = lax.broadcasted_iota(jnp.int32, (BS, BS), 0)
    lane = lax.broadcasted_iota(jnp.int32, (1, BS), 1)

    def chunk(c, unused):
        slot = (sub + c * BS).astype(F32)

        def line(r, total):
            hit = place[pl.ds(r, 1), :] == slot
            return total + jnp.where(hit, value[pl.ds(r, 1), :], 0.0)

        total = lax.fori_loop(0, at, line, jnp.zeros((BS, BS), F32), unroll=4)
        found = jnp.sum(total.T, axis=0, keepdims=True).astype(jnp.int32)
        out_ref[pl.ds(c, 1), :] = jnp.where(lane + c * BS < count, found, sz.own)
        return unused

    lax.fori_loop(0, lax.shift_right_logical(count + BS - 1, 7), chunk, 0)


def sweep(list_ref, count_ref, lhs_ref, rhs_ref, vec_ref, acc, acc_ones=None):
    acc[...] = jnp.zeros_like(acc)
    if acc_ones is not None:
        acc_ones[...] = jnp.zeros_like(acc_ones)

    def group(g, unused):
        for u in range(UNROLL):
            entry = list_ref[g * UNROLL + u]
            i = jnp.bitwise_and(entry, 255)
            j = lax.shift_right_logical(entry, 8)
            rows = pl.ds(pl.multiple_of(i * BS, BS), BS)
            squared = jnp.dot(
                lhs_ref[rows, :DEPTH],
                rhs_ref[pl.ds(pl.multiple_of(j * DEPTH, DEPTH), DEPTH), :],
                preferred_element_type=F32,
            )
            squared = jnp.maximum(squared, 1e-20)
            remain = jnp.maximum(4.0 - squared * lax.rsqrt(squared), 0.0)
            twice = remain * remain
            tile = twice * twice * (5.0 - remain)
            if acc_ones is not None:
                acc_ones[rows, :] += tile
            acc[rows, :] += tile * vec_ref[pl.ds(j, 1), :]
        return unused

    groups = lax.div(count_ref[0] + (UNROLL - 1), UNROLL)
    lax.fori_loop(0, groups, group, 0)


def finish(sz, acc, out_ref):
    unit = jnp.ones((8, BS), BF16)
    across = (((1,), (1,)), ((), ()))
    for i in range(sz.own):
        whole = acc[i * BS : (i + 1) * BS, :]
        high = whole.astype(BF16)
        low = (whole - high.astype(F32)).astype(BF16)
        y = lax.dot_general(unit, high, across, preferred_element_type=F32)
        y = y + lax.dot_general(unit, low, across, preferred_element_type=F32)
        out_ref[i : i + 1, :] = y[0:1, :] * sz.scale


def total_of(x):
    return jnp.sum(jnp.sum(x, axis=0, keepdims=True), axis=1, keepdims=True)


def first_kernel(sz, coord_codes, *refs):
    list_ref, count_ref, lhs_ref, nugget_ref = refs[:4]
    pieces = len(coord_codes)
    coord_refs = refs[4 : 4 + pieces]
    obs_refs = refs[4 + pieces : 4 + 2 * pieces]
    rhs_ref, obs_ref, diag_ref, mapped_ref, norm_ref, acc, acc_ones, total_row = refs[4 + 2 * pieces :]
    blk, rep = lax.axis_index("blk"), lax.axis_index("rep")
    unit = jnp.ones((1, BS), F32)
    for (z, r), coord_ref, piece_ref in zip(coord_codes, coord_refs, obs_refs):
        rows = piece_ref.shape[0]
        first = jnp.bitwise_xor(blk, z) * sz.local_blocks
        if r is not None:
            first = first + jnp.bitwise_xor(rep, r) * rows
        first = pl.multiple_of(first, 8)
        obs_ref[pl.ds(first, rows), :] = piece_ref[...]

        def one(k, unused, coord_ref=coord_ref, first=first):
            x = (coord_ref[:, pl.ds(pl.multiple_of(k * BS, BS), BS)] - 0.5) * (4.0 / SUPPORT)
            norm = jnp.sum(x * x, axis=0, keepdims=True)
            h, m, l = split3(jnp.concatenate([-2.0 * x, norm, unit, jnp.zeros((3, BS), F32)], axis=0))
            feats = jnp.concatenate([h, m, h, m, l, h], axis=0).astype(BF16)
            rhs_ref[pl.ds(pl.multiple_of((first + k) * DEPTH, DEPTH), DEPTH), :] = feats
            return unused

        lax.fori_loop(0, rows, one, 0, unroll=4)
    sweep(list_ref, count_ref, lhs_ref, rhs_ref, obs_ref, acc, acc_ones)
    finish(sz, acc_ones, total_row)
    finish(sz, acc, mapped_ref)
    quarter = lax.axis_index("col") * sz.reps + rep
    diag = nugget_ref[pl.ds(pl.multiple_of(quarter * sz.own, 8), sz.own), :] + total_row[...]
    diag_ref[...] = diag
    mapped_ref[...] += diag * obs_ref[pl.ds(pl.multiple_of(sz.me() * sz.own, 8), sz.own), :]
    norm_ref[...] = jnp.broadcast_to(total_of(obs_ref[...] * obs_ref[...]), (8, BS))


def step_kernel(sz, codes, last, *refs):
    list_ref, count_ref, lhs_ref, rhs_ref, diag_ref, norm_ref, field_ref, resid_ref, dirn_ref = refs[:9]
    pieces = refs[9 : 9 + len(codes)]
    rest = refs[9 + len(codes) :]
    mapped_ref, next_norm_ref, next_field_ref, next_resid_ref, next_dirn_ref = rest[:5]
    if last:
        dot_ref, mapped, dirn, acc = rest[5:]
    else:
        mapped, acc = rest[5:]
        dirn = next_dirn_ref
    me = sz.me()
    assemble(pieces, codes, me, sz.own, mapped)
    norm = norm_ref[0:1, 0:1]
    step = norm / total_of(dirn_ref[...] * mapped[...])
    resid = resid_ref[...] - step * mapped[...]
    next_norm = total_of(resid * resid)
    dirn[...] = resid + (next_norm / norm) * dirn_ref[...]
    next_norm_ref[...] = jnp.broadcast_to(next_norm, (8, BS))
    home = pl.ds(pl.multiple_of(lax.axis_index("blk") * sz.local_blocks, 8), sz.local_blocks)
    own = pl.ds(pl.multiple_of(me * sz.own, 8), sz.own)
    field = step * dirn_ref[home, :]
    if last:
        next_field_ref[...] = field_ref[...] + field
        next_resid_ref[...] = resid_ref[home, :] - step * mapped[home, :]
        next_dirn_ref[...] = dirn[home, :]
    else:
        next_field_ref[...] = field
        next_resid_ref[...] = resid
    sweep(list_ref, count_ref, lhs_ref, rhs_ref, dirn, acc)
    finish(sz, acc, mapped_ref)
    mapped_ref[...] += diag_ref[...] * dirn[own, :]
    if last:
        dot_ref[...] = jnp.broadcast_to(total_of(mapped_ref[...] * dirn[own, :]), (8, BS))


def last_kernel(sz, dots, *refs):
    norm_ref, field_ref, resid_ref, dirn_ref = refs[:4]
    pieces = refs[4 : 4 + sz.plane]
    dot_refs = refs[4 + sz.plane : 4 + sz.plane + dots]
    out_field_ref, out_resid_ref, mapped = refs[4 + sz.plane + dots :]
    quarter = lax.axis_index("col") * sz.reps + lax.axis_index("rep")
    assemble(pieces, [[s] for s in range(sz.plane)], quarter, sz.own, mapped)
    product = jnp.zeros((1, BS), F32)
    for ref in dot_refs:
        for k in range(ref.shape[0] // 8):
            product = product + ref[8 * k : 8 * k + 1, :]
    step = norm_ref[0:1, :] / product
    out_field_ref[...] = field_ref[...] + step * dirn_ref[...]
    out_resid_ref[...] = resid_ref[...] - step * mapped[...]


def call(kernel, in_specs, shapes, out_specs, scratch, flops, *args):
    return pl.pallas_call(
        kernel,
        in_specs=in_specs,
        out_shape=shapes,
        out_specs=out_specs,
        scratch_shapes=scratch,
        compiler_params=PARAMS,
        cost_estimate=pl.CostEstimate(flops=flops, bytes_accessed=1 << 20, transcendentals=0),
    )(*args)


def array(*shape, dtype=F32):
    return jax.ShapeDtypeStruct(shape, dtype)


def local(coords, observations, nugget, tile_pairs, tile_live):
    sz = Sizes(observations.shape[0], tile_pairs.shape[1])
    own, blocks, home = sz.own, sz.blocks, sz.local_blocks
    alive = jnp.arange(sz.slots, dtype=jnp.int32) < tile_live[0]
    pairs = jnp.where(alive, tile_pairs, -1).reshape(2 * sz.slots // BS, BS)
    pair_arrays, codes = spread(pairs, sz)

    rep = lax.axis_index("rep")
    obs_rows = observations.reshape(home, BS)
    half = sz.points // sz.reps
    part = lax.dynamic_slice_in_dim(coords, rep * half, half, axis=1)
    obs_part = lax.dynamic_slice_in_dim(obs_rows, rep * (home // sz.reps), home // sz.reps, axis=0)
    coord_arrays, obs_arrays, coord_codes = [coords], [obs_rows], [(0, None)]
    for z in range(1, sz.blks):
        near, near_obs = swap(part, "blk", sz.blks, z), swap(obs_part, "blk", sz.blks, z)
        for r in range(sz.reps):
            coord_arrays.append(swap(near, "rep", sz.reps, r) if r else near)
            obs_arrays.append(swap(near_obs, "rep", sz.reps, r) if r else near_obs)
            coord_codes.append((z, r))

    lhs = call(
        functools.partial(lhs_kernel, sz),
        [VMEM],
        array((own + 1) * BS, BS, dtype=BF16),
        VMEM,
        [],
        10_000_000,
        coords,
    )
    lines = 2 * sz.slots // BS * sz.devs
    table, count = call(
        functools.partial(list_kernel, sz, codes),
        [VMEM] * len(pair_arrays),
        (array(sz.capacity // BS, BS, dtype=jnp.int32), array(1, dtype=jnp.int32)),
        (VMEM, SMEM),
        [pltpu.VMEM((lines, BS), jnp.int32)] * 2 + [pltpu.VMEM((lines, BS), F32)] * 2,
        10_000_000,
        *pair_arrays,
    )
    table = table.reshape(sz.capacity)
    tall = pltpu.VMEM(((own + 1) * BS, BS), F32)
    rhs, obs, diag, mapped, norm = call(
        functools.partial(first_kernel, sz, coord_codes),
        [SMEM, SMEM] + [VMEM] * (2 + 2 * len(coord_codes)),
        (
            array(blocks * DEPTH, BS, dtype=BF16),
            array(blocks, BS),
            array(own, BS),
            array(own, BS),
            array(8, BS),
        ),
        (VMEM,) * 5,
        [tall, tall, pltpu.VMEM((own, BS), F32)],
        100_000_000,
        table,
        count,
        lhs,
        nugget.reshape(home, BS),
        *coord_arrays,
        *obs_arrays,
    )
    field, resid, dirn = norm, obs, obs
    for sweep_index in range(1, ITERS):
        last = sweep_index + 1 == ITERS
        arrays, codes = spread(mapped, sz)
        kept = home if last else blocks
        whole = pltpu.VMEM((blocks, BS), F32)
        outs = [array(own, BS), array(8, BS), array(home, BS), array(kept, BS), array(kept, BS)]
        mapped, norm, field, resid, dirn, *dot = call(
            functools.partial(step_kernel, sz, codes, last),
            [SMEM, SMEM] + [VMEM] * (7 + len(arrays)),
            outs + [array(8, BS)] * last,
            [VMEM] * (len(outs) + last),
            [whole] * (1 + last) + [tall],
            100_000_000,
            table,
            count,
            lhs,
            rhs,
            diag,
            norm,
            field,
            resid,
            dirn,
            *arrays,
        )
    dots, unused = spread(dot[0], sz)
    mapped_arrays = [mapped] + [swap(mapped, PLANE, sz.plane, s) for s in range(1, sz.plane)]
    field, resid = call(
        functools.partial(last_kernel, sz, len(dots)),
        [VMEM] * (4 + len(mapped_arrays) + len(dots)),
        (array(home, BS), array(home, BS)),
        (VMEM, VMEM),
        [pltpu.VMEM((home, BS), F32)],
        100_000,
        norm,
        field,
        resid,
        dirn,
        *mapped_arrays,
        *dots,
    )
    return field.reshape(sz.points), resid.reshape(sz.points)


def solution(mesh):
    in_specs = (
        P(None, ("grp", "blk")),
        P(("grp", "blk")),
        P(("grp", "blk")),
        P(None, ("grp", "blk", "col", "rep")),
        P(("grp", "blk", "col", "rep")),
    )
    out_specs = (P(("grp", "blk")), P(("grp", "blk")))
    return jax.shard_map(local, mesh=mesh, in_specs=in_specs, out_specs=out_specs, check_vma=False)
```

time: 578 us -> 218 us (0.38); the launches traced: 568 us -> 217 us
  matrix products: 181 us -> 0 us
  waiting for transfers between devices: 199 us -> 28 us
  blocking collectives: 103 us -> 0 us
  starting transfers between devices: 0.25 us -> 96.6 us
  Pallas kernels: 0 us -> 85 us
  other arithmetic: 43.4 us -> 0.69 us
  between operations: 26 us -> 1.47 us
  local copies, waits for them, and re-layouts: 15.2 us -> 5.28 us
    dot_general x16 -> x0, matrix products: 181 us -> none  [the longest x4 108 us: apply_off(): forward = jnp.einsum('sac,sc->sa', tiles, col_vecs, precision=highest)]
    unnamed x9 -> x0, waiting for transfers between devices: 103 us -> none
    ppermute x0 -> x75, starting transfers between devices: none -> 96.6 us  [swap(): return lax.ppermute(x, axes, [(i, i ^ code) for i in range(count)])]
    psum x3 -> x0, waiting for transfers between devices: 95.7 us -> none  [apply_off(): joined = lax.psum(partial_value, ('col', 'rep'))]
    pallas_call x0 -> x6, Pallas kernels: none -> 85 us  [call(): pl.pallas_call(kernel, in_specs=in_specs, out_shape=shapes, out_specs=out...]
    all_gather x4 -> x0, blocking collectives: 66.4 us -> none  [the longest x3 42 us: mapped_of(): whole = lax.all_gather(vector_in, 'blk', axis=0, tiled=True)]
    psum x3 -> x0, blocking collectives: 37 us -> none  [pair_totals(): lax.psum((jnp.sum(residual * residual), jnp.sum(residual * mapped)), 'blk')]
    ppermute x0 -> x75, waiting for transfers between devices: none -> 28 us  [swap(): return lax.ppermute(x, axes, [(i, i ^ code) for i in range(count)])]
  transfers between devices with their start and end apart: 6 -> 75, of which waited for: 6 -> 13; matrix products, arithmetic and copies ran while one was open for 0% -> 1% of each run, Pallas kernels for 0% -> 1%
where the time goes in v1:
time: 218 us; the launch traced here: 217 us
  starting transfers between devices  96.6 us (44%)
  Pallas kernels  85 us (39%)
  waiting for transfers between devices  28 us (13%)
  local copies, waits for them, and re-layouts  5.28 us (2%)
    ppermute x75, starting transfers between devices, swap(): return lax.ppermute(x, axes, [(i, i ^ code) for i in range(count)])  96.6 us
    pallas_call x6, Pallas kernels, call(): pl.pallas_call(kernel, in_specs=in_specs, out_shape=shapes, out_specs=out...  85 us
    ppermute x75, waiting for transfers between devices, swap(): return lax.ppermute(x, axes, [(i, i ^ code) for i in range(count)])  28 us
  transfers between devices with their start and end apart: 75, of which 13 were waited for; matrix products, arithmetic and copies ran while one was open for 1% of the time, Pallas kernels for 1%

profile of v1, /device:TPU:0, one launch (start us, length us, event | category | flops | bytes accessed | tf_op | source)
XLA Modules:
  0.0 217.1 jit_solution(5654805899944653666)
XLA Ops:
  2.0 5.4 %collective-permute-start.14 = (s32[4,128]{1,0:T(4,128)S(1)}, s32[4,128]{1,0:T(4,128)S(1)}, u32[]{:S(2)}, u32[]{:S(2)}) collective-permute-start(s32[4,128]{1,0:T(4,128)S(1)} %reshape.22.refs_0_), channel_id=1, source_target_pairs={{0,15},{1,14},{2,13},{3,12},{4,11},{5,10},{6,9},{7,8},{8,7},{9,6},... | collective-permute-start | bytes 6152 | tf_op jit(solution)/shard_map/ppermute | solution.py:46
  8.0 3.2 %collective-permute-start.12 = (s32[4,128]{1,0:T(4,128)S(1)}, s32[4,128]{1,0:T(4,128)S(1)}, u32[]{:S(2)}, u32[]{:S(2)}) collective-permute-start(s32[4,128]{1,0:T(4,128)S(1)} %reshape.22.refs_0_), channel_id=1, source_target_pairs={{0,13},{1,12},{2,15},{3,14},{4,9},{5,8},{6,11},{7,10},{8,5},{9,4},... | collective-permute-start | bytes 6152 | tf_op jit(solution)/shard_map/ppermute | solution.py:46
  11.5 3.6 %collective-permute-start.9 = (s32[4,128]{1,0:T(4,128)S(1)}, s32[4,128]{1,0:T(4,128)S(1)}, u32[]{:S(2)}, u32[]{:S(2)}) collective-permute-start(s32[4,128]{1,0:T(4,128)S(1)} %reshape.22.refs_0_), channel_id=1, source_target_pairs={{0,10},{1,11},{2,8},{3,9},{4,14},{5,15},{6,12},{7,13},{8,2},{9,3},... | collective-permute-start | bytes 6152 | tf_op jit(solution)/shard_map/ppermute | solution.py:46
  15.1 2.6 %collective-permute-start.7 = (s32[4,128]{1,0:T(4,128)S(1)}, s32[4,128]{1,0:T(4,128)S(1)}, u32[]{:S(2)}, u32[]{:S(2)}) collective-permute-start(s32[4,128]{1,0:T(4,128)S(1)} %reshape.22.refs_0_), channel_id=1, source_target_pairs={{0,8},{1,9},{2,10},{3,11},{4,12},{5,13},{6,14},{7,15},{8,0},{9,1},... | collective-permute-start | bytes 6152 | tf_op jit(solution)/shard_map/ppermute | solution.py:46
  17.7 1.9 collective-permute-start.6
  20.4 1.2 collective-permute-start.4
  22.1 1.0 collective-permute-start.2
  23.1 0.9 constant_dynamic-slice_fusion.1
  24.1 0.9 collective-permute-start.1
  25.0 3.6 %collective-permute-start.19 = (f32[3,8192]{1,0:T(4,128)S(1)}, f32[3,8192]{1,0:T(4,128)S(1)}, u32[]{:S(2)}, u32[]{:S(2)}) collective-permute-start(f32[3,8192]{1,0:T(4,128)S(1)} %constant_dynamic-slice_fusion.1), channel_id=1, source_target_pairs={{0,12},{4,8},{8,4},{12,0},{1,13},{5,9},{9,5},{13,1},{2,14},{6,10},... | collective-permute-start | bytes 294920 | tf_op jit(solution)/shard_map/ppermute | solution.py:46
  30.2 3.5 %collective-permute-start.25 = (f32[64,128]{1,0:T(8,128)S(1)}, f32[64,128]{1,0:T(8,128)S(1)}, u32[]{:S(2)}, u32[]{:S(2)}) collective-permute-start(f32[64,128]{1,0:T(8,128)S(1)} %constant_dynamic-slice_fusion), channel_id=1, source_target_pairs={{0,12},{4,8},{8,4},{12,0},{1,13},{5,9},{9,5},{13,1},{2,14},{6,10},... | collective-permute-start | bytes 98312 | tf_op jit(solution)/shard_map/ppermute | solution.py:46
  33.8 8.3 %collective-permute-done.17.refs_7_ = f32[3,8192]{1,0:T(4,128)S(1)} collective-permute-done((f32[3,8192]{1,0:T(4,128)S(1)}, f32[3,8192]{1,0:T(4,128)S(1)}, u32[]{:S(2)}, u32[]{:S(2)}) %collective-permute-start.17) | collective-permute-done | bytes 98336 | tf_op jit(solution)/shard_map/ppermute | solution.py:46
  43.2 3.4 %collective-permute-done.21.refs_12_ = f32[64,128]{1,0:T(8,128)S(1)} collective-permute-done((f32[64,128]{1,0:T(8,128)S(1)}, f32[64,128]{1,0:T(8,128)S(1)}, u32[]{:S(2)}, u32[]{:S(2)}) %collective-permute-start.21) | collective-permute-done | bytes 32800 | tf_op jit(solution)/shard_map/ppermute | solution.py:46
  47.1 0.9 copy-done
  48.4 2.5 %shard_map.68 = (s32[16,128]{1,0:T(8,128)S(1)}, s32[1]{0:T(128)}) custom-call(s32[4,128]{1,0:T(4,128)S(1)} %reshape.22.refs_0_, s32[4,128]{1,0:T(4,128)S(1)} %collective-permute-done.refs_1_, s32[4,128]{1,0:T(4,128)S(1)} %collective-permute-done.1.refs_2_, s32[4,128]{1,0:T(4,128)S(1)} %collective-permute-done.2.refs_3_, ...), custom_call_target="tpu_custom_call" | custom-call | flops 10000000 | bytes 1048576 | tf_op jit(solution)/shard_map/pallas_call | solution.py:264
  51.0 0.9 copy-done.1
  51.9 0.8 copy-done.2
  53.6 29.7 %shard_map.70 = (bf16[24576,128]{1,0:T(8,128)(2,1)}, f32[512,128]{1,0:T(8,128)S(1)}, f32[32,128]{1,0:T(8,128)S(1)}, f32[32,128]{1,0:T(8,128)S(1)}, f32[8,128]{1,0:T(8,128)S(1)}) custom-call(s32[2048]{0:T(1024)S(1)} %bitcast.9, s32[1]{0:T(128)} %get-tuple-element.23.refs_1_, bf16[4224,128]{1,0:T(8,128)(2,1)S(1)} %shard_map.69.refs_2_, ...), custom_call_target="tpu_custom_call" | custom-call | flops 100000000 | bytes 1048576 | tf_op jit(solution)/shard_map/pallas_call | solution.py:264
  83.3 5.8 %collective-permute-start.41 = (f32[32,128]{1,0:T(8,128)S(1)}, f32[32,128]{1,0:T(8,128)S(1)}, u32[]{:S(2)}, u32[]{:S(2)}) collective-permute-start(f32[32,128]{1,0:T(8,128)S(1)} %get-tuple-element.28.refs_9_), channel_id=1, source_target_pairs={{0,15},{1,14},{2,13},{3,12},{4,11},{5,10},{6,9},{7,8},{8,7},{9,6},... | collective-permute-start | bytes 49160 | tf_op jit(solution)/shard_map/ppermute | solution.py:46
  89.0 3.6 %collective-permute-start.38 = (f32[32,128]{1,0:T(8,128)S(1)}, f32[32,128]{1,0:T(8,128)S(1)}, u32[]{:S(2)}, u32[]{:S(2)}) collective-permute-start(f32[32,128]{1,0:T(8,128)S(1)} %get-tuple-element.28.refs_9_), channel_id=1, source_target_pairs={{0,12},{1,13},{2,14},{3,15},{4,8},{5,9},{6,10},{7,11},{8,4},{9,5},... | collective-permute-start | bytes 49160 | tf_op jit(solution)/shard_map/ppermute | solution.py:46
  92.6 3.5 %collective-permute-start.36 = (f32[32,128]{1,0:T(8,128)S(1)}, f32[32,128]{1,0:T(8,128)S(1)}, u32[]{:S(2)}, u32[]{:S(2)}) collective-permute-start(f32[32,128]{1,0:T(8,128)S(1)} %get-tuple-element.28.refs_9_), channel_id=1, source_target_pairs={{0,10},{1,11},{2,8},{3,9},{4,14},{5,15},{6,12},{7,13},{8,2},{9,3},... | collective-permute-start | bytes 49160 | tf_op jit(solution)/shard_map/ppermute | solution.py:46
  96.5 2.3 %collective-permute-start.34 = (f32[32,128]{1,0:T(8,128)S(1)}, f32[32,128]{1,0:T(8,128)S(1)}, u32[]{:S(2)}, u32[]{:S(2)}) collective-permute-start(f32[32,128]{1,0:T(8,128)S(1)} %get-tuple-element.28.refs_9_), channel_id=1, source_target_pairs={{0,8},{1,9},{2,10},{3,11},{4,12},{5,13},{6,14},{7,15},{8,0},{9,1},... | collective-permute-start | bytes 49160 | tf_op jit(solution)/shard_map/ppermute | solution.py:46
  98.8 2.4 %collective-permute-start.33 = (f32[32,128]{1,0:T(8,128)S(1)}, f32[32,128]{1,0:T(8,128)S(1)}, u32[]{:S(2)}, u32[]{:S(2)}) collective-permute-start(f32[32,128]{1,0:T(8,128)S(1)} %get-tuple-element.28.refs_9_), channel_id=1, source_target_pairs={{0,7},{1,6},{2,5},{3,4},{4,3},{5,2},{6,1},{7,0},{8,15},{9,14},{10,... | collective-permute-start | bytes 49160 | tf_op jit(solution)/shard_map/ppermute | solution.py:46
  101.6 1.1 collective-permute-start.31
  103.4 1.3 collective-permute-start.29
  105.1 0.9 collective-permute-done.32.refs_15_
  106.5 1.9 collective-permute-done.28.refs_11_
  108.4 25.9 %shard_map.71 = (f32[32,128]{1,0:T(8,128)S(1)}, f32[8,128]{1,0:T(8,128)S(1)}, f32[128,128]{1,0:T(8,128)S(1)}, f32[512,128]{1,0:T(8,128)S(1)}, f32[512,128]{1,0:T(8,128)S(1)}) custom-call(s32[2048]{0:T(1024)S(1)} %bitcast.10, s32[1]{0:T(128)} %get-tuple-element.23.refs_1_, bf16[4224,128]{1,0:T(8,128)(2,1)S(1)} %shard_map.69.refs_2_, ...), custom_call_target="tpu_custom_call" | custom-call | flops 100000000 | bytes 1048576 | tf_op jit(solution)/shard_map/pallas_call | solution.py:264
  134.3 5.4 %collective-permute-start.56 = (f32[32,128]{1,0:T(8,128)S(1)}, f32[32,128]{1,0:T(8,128)S(1)}, u32[]{:S(2)}, u32[]{:S(2)}) collective-permute-start(f32[32,128]{1,0:T(8,128)S(1)} %get-tuple-element.33.refs_9_), channel_id=1, source_target_pairs={{0,15},{1,14},{2,13},{3,12},{4,11},{5,10},{6,9},{7,8},{8,7},{9,6},... | collective-permute-start | bytes 49160 | tf_op jit(solution)/shard_map/ppermute | solution.py:46
  139.7 3.6 %collective-permute-start.53 = (f32[32,128]{1,0:T(8,128)S(1)}, f32[32,128]{1,0:T(8,128)S(1)}, u32[]{:S(2)}, u32[]{:S(2)}) collective-permute-start(f32[32,128]{1,0:T(8,128)S(1)} %get-tuple-element.33.refs_9_), channel_id=1, source_target_pairs={{0,12},{1,13},{2,14},{3,15},{4,8},{5,9},{6,10},{7,11},{8,4},{9,5},... | collective-permute-start | bytes 49160 | tf_op jit(solution)/shard_map/ppermute | solution.py:46
  143.3 3.5 %collective-permute-start.51 = (f32[32,128]{1,0:T(8,128)S(1)}, f32[32,128]{1,0:T(8,128)S(1)}, u32[]{:S(2)}, u32[]{:S(2)}) collective-permute-start(f32[32,128]{1,0:T(8,128)S(1)} %get-tuple-element.33.refs_9_), channel_id=1, source_target_pairs={{0,10},{1,11},{2,8},{3,9},{4,14},{5,15},{6,12},{7,13},{8,2},{9,3},... | collective-permute-start | bytes 49160 | tf_op jit(solution)/shard_map/ppermute | solution.py:46
  147.1 2.3 %collective-permute-start.49 = (f32[32,128]{1,0:T(8,128)S(1)}, f32[32,128]{1,0:T(8,128)S(1)}, u32[]{:S(2)}, u32[]{:S(2)}) collective-permute-start(f32[32,128]{1,0:T(8,128)S(1)} %get-tuple-element.33.refs_9_), channel_id=1, source_target_pairs={{0,8},{1,9},{2,10},{3,11},{4,12},{5,13},{6,14},{7,15},{8,0},{9,1},... | collective-permute-start | bytes 49160 | tf_op jit(solution)/shard_map/ppermute | solution.py:46
  149.5 2.4 %collective-permute-start.48 = (f32[32,128]{1,0:T(8,128)S(1)}, f32[32,128]{1,0:T(8,128)S(1)}, u32[]{:S(2)}, u32[]{:S(2)}) collective-permute-start(f32[32,128]{1,0:T(8,128)S(1)} %get-tuple-element.33.refs_9_), channel_id=1, source_target_pairs={{0,7},{1,6},{2,5},{3,4},{4,3},{5,2},{6,1},{7,0},{8,15},{9,14},{10,... | collective-permute-start | bytes 49160 | tf_op jit(solution)/shard_map/ppermute | solution.py:46
  152.2 1.1 collective-permute-start.46
  154.0 1.3 collective-permute-start.44
  155.7 0.9 collective-permute-done.47.refs_15_
  157.1 1.9 collective-permute-done.43.refs_11_
  159.0 25.9 %shard_map.72 = (f32[32,128]{1,0:T(8,128)S(1)}, f32[8,128]{1,0:T(8,128)S(1)}, f32[128,128]{1,0:T(8,128)S(1)}, f32[128,128]{1,0:T(8,128)S(1)}, f32[128,128]{1,0:T(8,128)S(1)}, /*index=5*/f32[8,128]{1,0:T(8,128)S(1)}) custom-call(s32[2048]{0:T(1024)S(1)} %bitcast.11, s32[1]{0:T(128)} %get-tuple-element.23.refs_1_, bf16[4224,128]{1,0:T(8,128)(2,1)S(1)} %shard_map.69.refs_2_, ...), custom_call_target="tpu_custom_call" | custom-call | flops 100000000 | bytes 1048576 | tf_op jit(solution)/shard_map/pallas_call | solution.py:264
  185.0 5.4 %collective-permute-start.74 = (f32[8,128]{1,0:T(8,128)S(1)}, f32[8,128]{1,0:T(8,128)S(1)}, u32[]{:S(2)}, u32[]{:S(2)}) collective-permute-start(f32[8,128]{1,0:T(8,128)S(1)} %get-tuple-element.39.refs_8_), channel_id=1, source_target_pairs={{0,15},{1,14},{2,13},{3,12},{4,11},{5,10},{6,9},{7,8},{8,7},{9,6},... | collective-permute-start | bytes 12296 | tf_op jit(solution)/shard_map/ppermute | solution.py:46
  190.4 3.6 %collective-permute-start.71 = (f32[8,128]{1,0:T(8,128)S(1)}, f32[8,128]{1,0:T(8,128)S(1)}, u32[]{:S(2)}, u32[]{:S(2)}) collective-permute-start(f32[8,128]{1,0:T(8,128)S(1)} %get-tuple-element.39.refs_8_), channel_id=1, source_target_pairs={{0,12},{1,13},{2,14},{3,15},{4,8},{5,9},{6,10},{7,11},{8,4},{9,5},... | collective-permute-start | bytes 12296 | tf_op jit(solution)/shard_map/ppermute | solution.py:46
  194.0 3.5 %collective-permute-start.69 = (f32[8,128]{1,0:T(8,128)S(1)}, f32[8,128]{1,0:T(8,128)S(1)}, u32[]{:S(2)}, u32[]{:S(2)}) collective-permute-start(f32[8,128]{1,0:T(8,128)S(1)} %get-tuple-element.39.refs_8_), channel_id=1, source_target_pairs={{0,10},{1,11},{2,8},{3,9},{4,14},{5,15},{6,12},{7,13},{8,2},{9,3},... | collective-permute-start | bytes 12296 | tf_op jit(solution)/shard_map/ppermute | solution.py:46
  197.8 2.3 %collective-permute-start.67 = (f32[8,128]{1,0:T(8,128)S(1)}, f32[8,128]{1,0:T(8,128)S(1)}, u32[]{:S(2)}, u32[]{:S(2)}) collective-permute-start(f32[8,128]{1,0:T(8,128)S(1)} %get-tuple-element.39.refs_8_), channel_id=1, source_target_pairs={{0,8},{1,9},{2,10},{3,11},{4,12},{5,13},{6,14},{7,15},{8,0},{9,1},... | collective-permute-start | bytes 12296 | tf_op jit(solution)/shard_map/ppermute | solution.py:46
  200.2 2.4 %collective-permute-start.66 = (f32[8,128]{1,0:T(8,128)S(1)}, f32[8,128]{1,0:T(8,128)S(1)}, u32[]{:S(2)}, u32[]{:S(2)}) collective-permute-start(f32[8,128]{1,0:T(8,128)S(1)} %get-tuple-element.39.refs_8_), channel_id=1, source_target_pairs={{0,7},{1,6},{2,5},{3,4},{4,3},{5,2},{6,1},{7,0},{8,15},{9,14},{10,... | collective-permute-start | bytes 12296 | tf_op jit(solution)/shard_map/ppermute | solution.py:46
  202.8 1.8 collective-permute-start.58
  204.6 1.2 collective-permute-start.65
  206.1 3.1 %collective-permute-done.65.refs_14_ = f32[8,128]{1,0:T(8,128)S(1)} collective-permute-done((f32[8,128]{1,0:T(8,128)S(1)}, f32[8,128]{1,0:T(8,128)S(1)}, u32[]{:S(2)}, u32[]{:S(2)}) %collective-permute-start.65) | collective-permute-done | bytes 4128 | tf_op jit(solution)/shard_map/ppermute | solution.py:46
  209.7 3.1 %collective-permute-done.63.refs_12_ = f32[8,128]{1,0:T(8,128)S(1)} collective-permute-done((f32[8,128]{1,0:T(8,128)S(1)}, f32[8,128]{1,0:T(8,128)S(1)}, u32[]{:S(2)}, u32[]{:S(2)}) %collective-permute-start.63) | collective-permute-done | bytes 4128 | tf_op jit(solution)/shard_map/ppermute | solution.py:46
  213.0 3.4 %collective-permute-done.61.refs_10_ = f32[8,128]{1,0:T(8,128)S(1)} collective-permute-done((f32[8,128]{1,0:T(8,128)S(1)}, f32[8,128]{1,0:T(8,128)S(1)}, u32[]{:S(2)}, u32[]{:S(2)}) %collective-permute-start.61) | collective-permute-done | bytes 4128 | tf_op jit(solution)/shard_map/ppermute | solution.py:46
  (121 shorter events, 14.7 us)
Async XLA Ops:
  2.0 9.5 %collective-permute-start.14 = (s32[4,128]{1,0:T(4,128)S(1)}, s32[4,128]{1,0:T(4,128)S(1)}, u32[]{:S(2)}, u32[]{:S(2)}) collective-permute-start(s32[4,128]{1,0:T(4,128)S(1)} %reshape.22.refs_0_), channel_id=1, source_target_pairs={{0,15},{1,14},{2,13},{3,12},{4,11},{5,10},{6,9},{7,8},{8,7},{9,6},... | collective-permute-start | bytes 6152 | tf_op jit(solution)/shard_map/ppermute | solution.py:46
  7.4 7.7 %collective-permute-start.13 = (s32[4,128]{1,0:T(4,128)S(1)}, s32[4,128]{1,0:T(4,128)S(1)}, u32[]{:S(2)}, u32[]{:S(2)}) collective-permute-start(s32[4,128]{1,0:T(4,128)S(1)} %reshape.22.refs_0_), channel_id=1, source_target_pairs={{0,14},{1,15},{2,12},{3,13},{4,10},{5,11},{6,8},{7,9},{8,6},{9,7},... | collective-permute-start | bytes 6152 | tf_op jit(solution)/shard_map/ppermute | solution.py:46
  8.0 7.1 %collective-permute-start.12 = (s32[4,128]{1,0:T(4,128)S(1)}, s32[4,128]{1,0:T(4,128)S(1)}, u32[]{:S(2)}, u32[]{:S(2)}) collective-permute-start(s32[4,128]{1,0:T(4,128)S(1)} %reshape.22.refs_0_), channel_id=1, source_target_pairs={{0,13},{1,12},{2,15},{3,14},{4,9},{5,8},{6,11},{7,10},{8,5},{9,4},... | collective-permute-start | bytes 6152 | tf_op jit(solution)/shard_map/ppermute | solution.py:46
  11.2 6.5 %collective-permute-start.11 = (s32[4,128]{1,0:T(4,128)S(1)}, s32[4,128]{1,0:T(4,128)S(1)}, u32[]{:S(2)}, u32[]{:S(2)}) collective-permute-start(s32[4,128]{1,0:T(4,128)S(1)} %reshape.22.refs_0_), channel_id=1, source_target_pairs={{0,12},{1,13},{2,14},{3,15},{4,8},{5,9},{6,10},{7,11},{8,4},{9,5},... | collective-permute-start | bytes 6152 | tf_op jit(solution)/shard_map/ppermute | solution.py:46
  11.5 8.1 %collective-permute-start.10 = (s32[4,128]{1,0:T(4,128)S(1)}, s32[4,128]{1,0:T(4,128)S(1)}, u32[]{:S(2)}, u32[]{:S(2)}) collective-permute-start(s32[4,128]{1,0:T(4,128)S(1)} %reshape.22.refs_0_), channel_id=1, source_target_pairs={{0,11},{1,10},{2,9},{3,8},{4,15},{5,14},{6,13},{7,12},{8,3},{9,2},... | collective-permute-start | bytes 6152 | tf_op jit(solution)/shard_map/ppermute | solution.py:46
  11.5 8.9 %collective-permute-start.9 = (s32[4,128]{1,0:T(4,128)S(1)}, s32[4,128]{1,0:T(4,128)S(1)}, u32[]{:S(2)}, u32[]{:S(2)}) collective-permute-start(s32[4,128]{1,0:T(4,128)S(1)} %reshape.22.refs_0_), channel_id=1, source_target_pairs={{0,10},{1,11},{2,8},{3,9},{4,14},{5,15},{6,12},{7,13},{8,2},{9,3},... | collective-permute-start | bytes 6152 | tf_op jit(solution)/shard_map/ppermute | solution.py:46
  15.1 6.5 %collective-permute-start.8 = (s32[4,128]{1,0:T(4,128)S(1)}, s32[4,128]{1,0:T(4,128)S(1)}, u32[]{:S(2)}, u32[]{:S(2)}) collective-permute-start(s32[4,128]{1,0:T(4,128)S(1)} %reshape.22.refs_0_), channel_id=1, source_target_pairs={{0,9},{1,8},{2,11},{3,10},{4,13},{5,12},{6,15},{7,14},{8,1},{9,0},... | collective-permute-start | bytes 6152 | tf_op jit(solution)/shard_map/ppermute | solution.py:46
  15.1 7.0 %collective-permute-start.7 = (s32[4,128]{1,0:T(4,128)S(1)}, s32[4,128]{1,0:T(4,128)S(1)}, u32[]{:S(2)}, u32[]{:S(2)}) collective-permute-start(s32[4,128]{1,0:T(4,128)S(1)} %reshape.22.refs_0_), channel_id=1, source_target_pairs={{0,8},{1,9},{2,10},{3,11},{4,12},{5,13},{6,14},{7,15},{8,0},{9,1},... | collective-permute-start | bytes 6152 | tf_op jit(solution)/shard_map/ppermute | solution.py:46
  17.7 6.3 %collective-permute-start.6 = (s32[4,128]{1,0:T(4,128)S(1)}, s32[4,128]{1,0:T(4,128)S(1)}, u32[]{:S(2)}, u32[]{:S(2)}) collective-permute-start(s32[4,128]{1,0:T(4,128)S(1)} %reshape.22.refs_0_), channel_id=1, source_target_pairs={{0,7},{1,6},{2,5},{3,4},{4,3},{5,2},{6,1},{7,0},{8,15},{9,14},{10,... | collective-permute-start | bytes 6152 | tf_op jit(solution)/shard_map/ppermute | solution.py:46
  21.7 6.9 %collective-permute-start.3 = (s32[4,128]{1,0:T(4,128)S(1)}, s32[4,128]{1,0:T(4,128)S(1)}, u32[]{:S(2)}, u32[]{:S(2)}) collective-permute-start(s32[4,128]{1,0:T(4,128)S(1)} %reshape.22.refs_0_), channel_id=1, source_target_pairs={{0,4},{1,5},{2,6},{3,7},{4,0},{5,1},{6,2},{7,3},{8,12},{9,13},{10,... | collective-permute-start | bytes 6152 | tf_op jit(solution)/shard_map/ppermute | solution.py:46
  22.1 6.4 %collective-permute-start.2 = (s32[4,128]{1,0:T(4,128)S(1)}, s32[4,128]{1,0:T(4,128)S(1)}, u32[]{:S(2)}, u32[]{:S(2)}) collective-permute-start(s32[4,128]{1,0:T(4,128)S(1)} %reshape.22.refs_0_), channel_id=1, source_target_pairs={{0,3},{1,2},{2,1},{3,0},{4,7},{5,6},{6,5},{7,4},{8,11},{9,10},{10,... | collective-permute-start | bytes 6152 | tf_op jit(solution)/shard_map/ppermute | solution.py:46
  24.1 6.1 %collective-permute-start.1 = (s32[4,128]{1,0:T(4,128)S(1)}, s32[4,128]{1,0:T(4,128)S(1)}, u32[]{:S(2)}, u32[]{:S(2)}) collective-permute-start(s32[4,128]{1,0:T(4,128)S(1)} %reshape.22.refs_0_), channel_id=1, source_target_pairs={{0,2},{1,3},{2,0},{3,1},{4,6},{5,7},{6,4},{7,5},{8,10},{9,11},{10,... | collective-permute-start | bytes 6152 | tf_op jit(solution)/shard_map/ppermute | solution.py:46
  24.9 8.8 %collective-permute-start = (s32[4,128]{1,0:T(4,128)S(1)}, s32[4,128]{1,0:T(4,128)S(1)}, u32[]{:S(2)}, u32[]{:S(2)}) collective-permute-start(s32[4,128]{1,0:T(4,128)S(1)} %reshape.22.refs_0_), channel_id=1, source_target_pairs={{0,1},{1,0},{2,3},{3,2},{4,5},{5,4},{6,7},{7,6},{8,9},{9,8},{10,11... | collective-permute-start | bytes 6152 | tf_op jit(solution)/shard_map/ppermute | solution.py:46
  25.0 8.7 %collective-permute-start.19 = (f32[3,8192]{1,0:T(4,128)S(1)}, f32[3,8192]{1,0:T(4,128)S(1)}, u32[]{:S(2)}, u32[]{:S(2)}) collective-permute-start(f32[3,8192]{1,0:T(4,128)S(1)} %constant_dynamic-slice_fusion.1), channel_id=1, source_target_pairs={{0,12},{4,8},{8,4},{12,0},{1,13},{5,9},{9,5},{13,1},{2,14},{6,10},... | collective-permute-start | bytes 294920 | tf_op jit(solution)/shard_map/ppermute | solution.py:46
  28.6 13.6 %collective-permute-start.17 = (f32[3,8192]{1,0:T(4,128)S(1)}, f32[3,8192]{1,0:T(4,128)S(1)}, u32[]{:S(2)}, u32[]{:S(2)}) collective-permute-start(f32[3,8192]{1,0:T(4,128)S(1)} %constant_dynamic-slice_fusion.1), channel_id=1, source_target_pairs={{0,8},{4,12},{8,0},{12,4},{1,9},{5,13},{9,1},{13,5},{2,10},{6,14},... | collective-permute-start | bytes 294920 | tf_op jit(solution)/shard_map/ppermute | solution.py:46
  28.6 13.6 %collective-permute-start.15 = (f32[3,8192]{1,0:T(4,128)S(1)}, f32[3,8192]{1,0:T(4,128)S(1)}, u32[]{:S(2)}, u32[]{:S(2)}) collective-permute-start(f32[3,8192]{1,0:T(4,128)S(1)} %constant_dynamic-slice_fusion.1), channel_id=1, source_target_pairs={{0,4},{4,0},{8,12},{12,8},{1,5},{5,1},{9,13},{13,9},{2,6},{6,2},{1... | collective-permute-start | bytes 294920 | tf_op jit(solution)/shard_map/ppermute | solution.py:46
  30.2 12.5 %collective-permute-start.25 = (f32[64,128]{1,0:T(8,128)S(1)}, f32[64,128]{1,0:T(8,128)S(1)}, u32[]{:S(2)}, u32[]{:S(2)}) collective-permute-start(f32[64,128]{1,0:T(8,128)S(1)} %constant_dynamic-slice_fusion), channel_id=1, source_target_pairs={{0,12},{4,8},{8,4},{12,0},{1,13},{5,9},{9,5},{13,1},{2,14},{6,10},... | collective-permute-start | bytes 98312 | tf_op jit(solution)/shard_map/ppermute | solution.py:46
  33.7 9.5 %collective-permute-start.23 = (f32[64,128]{1,0:T(8,128)S(1)}, f32[64,128]{1,0:T(8,128)S(1)}, u32[]{:S(2)}, u32[]{:S(2)}) collective-permute-start(f32[64,128]{1,0:T(8,128)S(1)} %constant_dynamic-slice_fusion), channel_id=1, source_target_pairs={{0,8},{4,12},{8,0},{12,4},{1,9},{5,13},{9,1},{13,5},{2,10},{6,14},... | collective-permute-start | bytes 98312 | tf_op jit(solution)/shard_map/ppermute | solution.py:46
  33.7 17.2 %collective-permute-start.20 = (f32[3,8192]{1,0:T(4,128)S(1)}, f32[3,8192]{1,0:T(4,128)S(1)}, u32[]{:S(2)}, u32[]{:S(2)}) collective-permute-start(f32[3,8192]{1,0:T(4,128)S(1)} %collective-permute-done.19.refs_9_), channel_id=1, source_target_pairs={{0,1},{1,0},{2,3},{3,2},{4,5},{5,4},{6,7},{7,6},{8,9},{9,8},{10,11... | collective-permute-start | bytes 294920 | tf_op jit(solution)/shard_map/ppermute | solution.py:46
  42.2 8.8 %collective-permute-start.18 = (f32[3,8192]{1,0:T(4,128)S(1)}, f32[3,8192]{1,0:T(4,128)S(1)}, u32[]{:S(2)}, u32[]{:S(2)}) collective-permute-start(f32[3,8192]{1,0:T(4,128)S(1)} %collective-permute-done.17.refs_7_), channel_id=1, source_target_pairs={{0,1},{1,0},{2,3},{3,2},{4,5},{5,4},{6,7},{7,6},{8,9},{9,8},{10,11... | collective-permute-start | bytes 294920 | tf_op jit(solution)/shard_map/ppermute | solution.py:46
  42.2 8.8 %collective-permute-start.16 = (f32[3,8192]{1,0:T(4,128)S(1)}, f32[3,8192]{1,0:T(4,128)S(1)}, u32[]{:S(2)}, u32[]{:S(2)}) collective-permute-start(f32[3,8192]{1,0:T(4,128)S(1)} %collective-permute-done.15.refs_5_), channel_id=1, source_target_pairs={{0,1},{1,0},{2,3},{3,2},{4,5},{5,4},{6,7},{7,6},{8,9},{9,8},{10,11... | collective-permute-start | bytes 294920 | tf_op jit(solution)/shard_map/ppermute | solution.py:46
  83.3 9.4 %collective-permute-start.41 = (f32[32,128]{1,0:T(8,128)S(1)}, f32[32,128]{1,0:T(8,128)S(1)}, u32[]{:S(2)}, u32[]{:S(2)}) collective-permute-start(f32[32,128]{1,0:T(8,128)S(1)} %get-tuple-element.28.refs_9_), channel_id=1, source_target_pairs={{0,15},{1,14},{2,13},{3,12},{4,11},{5,10},{6,9},{7,8},{8,7},{9,6},... | collective-permute-start | bytes 49160 | tf_op jit(solution)/shard_map/ppermute | solution.py:46
  89.0 7.1 %collective-permute-start.40 = (f32[32,128]{1,0:T(8,128)S(1)}, f32[32,128]{1,0:T(8,128)S(1)}, u32[]{:S(2)}, u32[]{:S(2)}) collective-permute-start(f32[32,128]{1,0:T(8,128)S(1)} %get-tuple-element.28.refs_9_), channel_id=1, source_target_pairs={{0,14},{1,15},{2,12},{3,13},{4,10},{5,11},{6,8},{7,9},{8,6},{9,7},... | collective-permute-start | bytes 49160 | tf_op jit(solution)/shard_map/ppermute | solution.py:46
  89.0 7.5 %collective-permute-start.39 = (f32[32,128]{1,0:T(8,128)S(1)}, f32[32,128]{1,0:T(8,128)S(1)}, u32[]{:S(2)}, u32[]{:S(2)}) collective-permute-start(f32[32,128]{1,0:T(8,128)S(1)} %get-tuple-element.28.refs_9_), channel_id=1, source_target_pairs={{0,13},{1,12},{2,15},{3,14},{4,9},{5,8},{6,11},{7,10},{8,5},{9,4},... | collective-permute-start | bytes 49160 | tf_op jit(solution)/shard_map/ppermute | solution.py:46
  89.0 9.8 %collective-permute-start.38 = (f32[32,128]{1,0:T(8,128)S(1)}, f32[32,128]{1,0:T(8,128)S(1)}, u32[]{:S(2)}, u32[]{:S(2)}) collective-permute-start(f32[32,128]{1,0:T(8,128)S(1)} %get-tuple-element.28.refs_9_), channel_id=1, source_target_pairs={{0,12},{1,13},{2,14},{3,15},{4,8},{5,9},{6,10},{7,11},{8,4},{9,5},... | collective-permute-start | bytes 49160 | tf_op jit(solution)/shard_map/ppermute | solution.py:46
  92.6 8.6 %collective-permute-start.37 = (f32[32,128]{1,0:T(8,128)S(1)}, f32[32,128]{1,0:T(8,128)S(1)}, u32[]{:S(2)}, u32[]{:S(2)}) collective-permute-start(f32[32,128]{1,0:T(8,128)S(1)} %get-tuple-element.28.refs_9_), channel_id=1, source_target_pairs={{0,11},{1,10},{2,9},{3,8},{4,15},{5,14},{6,13},{7,12},{8,3},{9,2},... | collective-permute-start | bytes 49160 | tf_op jit(solution)/shard_map/ppermute | solution.py:46
  92.6 8.9 %collective-permute-start.36 = (f32[32,128]{1,0:T(8,128)S(1)}, f32[32,128]{1,0:T(8,128)S(1)}, u32[]{:S(2)}, u32[]{:S(2)}) collective-permute-start(f32[32,128]{1,0:T(8,128)S(1)} %get-tuple-element.28.refs_9_), channel_id=1, source_target_pairs={{0,10},{1,11},{2,8},{3,9},{4,14},{5,15},{6,12},{7,13},{8,2},{9,3},... | collective-permute-start | bytes 49160 | tf_op jit(solution)/shard_map/ppermute | solution.py:46
  96.1 6.5 %collective-permute-start.35 = (f32[32,128]{1,0:T(8,128)S(1)}, f32[32,128]{1,0:T(8,128)S(1)}, u32[]{:S(2)}, u32[]{:S(2)}) collective-permute-start(f32[32,128]{1,0:T(8,128)S(1)} %get-tuple-element.28.refs_9_), channel_id=1, source_target_pairs={{0,9},{1,8},{2,11},{3,10},{4,13},{5,12},{6,15},{7,14},{8,1},{9,0},... | collective-permute-start | bytes 49160 | tf_op jit(solution)/shard_map/ppermute | solution.py:46
  96.5 6.8 %collective-permute-start.34 = (f32[32,128]{1,0:T(8,128)S(1)}, f32[32,128]{1,0:T(8,128)S(1)}, u32[]{:S(2)}, u32[]{:S(2)}) collective-permute-start(f32[32,128]{1,0:T(8,128)S(1)} %get-tuple-element.28.refs_9_), channel_id=1, source_target_pairs={{0,8},{1,9},{2,10},{3,11},{4,12},{5,13},{6,14},{7,15},{8,0},{9,1},... | collective-permute-start | bytes 49160 | tf_op jit(solution)/shard_map/ppermute | solution.py:46
  134.3 9.0 %collective-permute-start.56 = (f32[32,128]{1,0:T(8,128)S(1)}, f32[32,128]{1,0:T(8,128)S(1)}, u32[]{:S(2)}, u32[]{:S(2)}) collective-permute-start(f32[32,128]{1,0:T(8,128)S(1)} %get-tuple-element.33.refs_9_), channel_id=1, source_target_pairs={{0,15},{1,14},{2,13},{3,12},{4,11},{5,10},{6,9},{7,8},{8,7},{9,6},... | collective-permute-start | bytes 49160 | tf_op jit(solution)/shard_map/ppermute | solution.py:46
  139.7 7.1 %collective-permute-start.55 = (f32[32,128]{1,0:T(8,128)S(1)}, f32[32,128]{1,0:T(8,128)S(1)}, u32[]{:S(2)}, u32[]{:S(2)}) collective-permute-start(f32[32,128]{1,0:T(8,128)S(1)} %get-tuple-element.33.refs_9_), channel_id=1, source_target_pairs={{0,14},{1,15},{2,12},{3,13},{4,10},{5,11},{6,8},{7,9},{8,6},{9,7},... | collective-permute-start | bytes 49160 | tf_op jit(solution)/shard_map/ppermute | solution.py:46
  139.7 7.5 %collective-permute-start.54 = (f32[32,128]{1,0:T(8,128)S(1)}, f32[32,128]{1,0:T(8,128)S(1)}, u32[]{:S(2)}, u32[]{:S(2)}) collective-permute-start(f32[32,128]{1,0:T(8,128)S(1)} %get-tuple-element.33.refs_9_), channel_id=1, source_target_pairs={{0,13},{1,12},{2,15},{3,14},{4,9},{5,8},{6,11},{7,10},{8,5},{9,4},... | collective-permute-start | bytes 49160 | tf_op jit(solution)/shard_map/ppermute | solution.py:46
  139.7 9.8 %collective-permute-start.53 = (f32[32,128]{1,0:T(8,128)S(1)}, f32[32,128]{1,0:T(8,128)S(1)}, u32[]{:S(2)}, u32[]{:S(2)}) collective-permute-start(f32[32,128]{1,0:T(8,128)S(1)} %get-tuple-element.33.refs_9_), channel_id=1, source_target_pairs={{0,12},{1,13},{2,14},{3,15},{4,8},{5,9},{6,10},{7,11},{8,4},{9,5},... | collective-permute-start | bytes 49160 | tf_op jit(solution)/shard_map/ppermute | solution.py:46
  143.2 8.6 %collective-permute-start.52 = (f32[32,128]{1,0:T(8,128)S(1)}, f32[32,128]{1,0:T(8,128)S(1)}, u32[]{:S(2)}, u32[]{:S(2)}) collective-permute-start(f32[32,128]{1,0:T(8,128)S(1)} %get-tuple-element.33.refs_9_), channel_id=1, source_target_pairs={{0,11},{1,10},{2,9},{3,8},{4,15},{5,14},{6,13},{7,12},{8,3},{9,2},... | collective-permute-start | bytes 49160 | tf_op jit(solution)/shard_map/ppermute | solution.py:46
  143.3 8.9 %collective-permute-start.51 = (f32[32,128]{1,0:T(8,128)S(1)}, f32[32,128]{1,0:T(8,128)S(1)}, u32[]{:S(2)}, u32[]{:S(2)}) collective-permute-start(f32[32,128]{1,0:T(8,128)S(1)} %get-tuple-element.33.refs_9_), channel_id=1, source_target_pairs={{0,10},{1,11},{2,8},{3,9},{4,14},{5,15},{6,12},{7,13},{8,2},{9,3},... | collective-permute-start | bytes 49160 | tf_op jit(solution)/shard_map/ppermute | solution.py:46
  146.8 6.5 %collective-permute-start.50 = (f32[32,128]{1,0:T(8,128)S(1)}, f32[32,128]{1,0:T(8,128)S(1)}, u32[]{:S(2)}, u32[]{:S(2)}) collective-permute-start(f32[32,128]{1,0:T(8,128)S(1)} %get-tuple-element.33.refs_9_), channel_id=1, source_target_pairs={{0,9},{1,8},{2,11},{3,10},{4,13},{5,12},{6,15},{7,14},{8,1},{9,0},... | collective-permute-start | bytes 49160 | tf_op jit(solution)/shard_map/ppermute | solution.py:46
  147.1 6.8 %collective-permute-start.49 = (f32[32,128]{1,0:T(8,128)S(1)}, f32[32,128]{1,0:T(8,128)S(1)}, u32[]{:S(2)}, u32[]{:S(2)}) collective-permute-start(f32[32,128]{1,0:T(8,128)S(1)} %get-tuple-element.33.refs_9_), channel_id=1, source_target_pairs={{0,8},{1,9},{2,10},{3,11},{4,12},{5,13},{6,14},{7,15},{8,0},{9,1},... | collective-permute-start | bytes 49160 | tf_op jit(solution)/shard_map/ppermute | solution.py:46
  185.0 9.0 %collective-permute-start.74 = (f32[8,128]{1,0:T(8,128)S(1)}, f32[8,128]{1,0:T(8,128)S(1)}, u32[]{:S(2)}, u32[]{:S(2)}) collective-permute-start(f32[8,128]{1,0:T(8,128)S(1)} %get-tuple-element.39.refs_8_), channel_id=1, source_target_pairs={{0,15},{1,14},{2,13},{3,12},{4,11},{5,10},{6,9},{7,8},{8,7},{9,6},... | collective-permute-start | bytes 12296 | tf_op jit(solution)/shard_map/ppermute | solution.py:46
  190.3 7.1 %collective-permute-start.73 = (f32[8,128]{1,0:T(8,128)S(1)}, f32[8,128]{1,0:T(8,128)S(1)}, u32[]{:S(2)}, u32[]{:S(2)}) collective-permute-start(f32[8,128]{1,0:T(8,128)S(1)} %get-tuple-element.39.refs_8_), channel_id=1, source_target_pairs={{0,14},{1,15},{2,12},{3,13},{4,10},{5,11},{6,8},{7,9},{8,6},{9,7},... | collective-permute-start | bytes 12296 | tf_op jit(solution)/shard_map/ppermute | solution.py:46
  190.4 7.5 %collective-permute-start.72 = (f32[8,128]{1,0:T(8,128)S(1)}, f32[8,128]{1,0:T(8,128)S(1)}, u32[]{:S(2)}, u32[]{:S(2)}) collective-permute-start(f32[8,128]{1,0:T(8,128)S(1)} %get-tuple-element.39.refs_8_), channel_id=1, source_target_pairs={{0,13},{1,12},{2,15},{3,14},{4,9},{5,8},{6,11},{7,10},{8,5},{9,4},... | collective-permute-start | bytes 12296 | tf_op jit(solution)/shard_map/ppermute | solution.py:46
  190.4 9.8 %collective-permute-start.71 = (f32[8,128]{1,0:T(8,128)S(1)}, f32[8,128]{1,0:T(8,128)S(1)}, u32[]{:S(2)}, u32[]{:S(2)}) collective-permute-start(f32[8,128]{1,0:T(8,128)S(1)} %get-tuple-element.39.refs_8_), channel_id=1, source_target_pairs={{0,12},{1,13},{2,14},{3,15},{4,8},{5,9},{6,10},{7,11},{8,4},{9,5},... | collective-permute-start | bytes 12296 | tf_op jit(solution)/shard_map/ppermute | solution.py:46
  194.0 8.6 %collective-permute-start.70 = (f32[8,128]{1,0:T(8,128)S(1)}, f32[8,128]{1,0:T(8,128)S(1)}, u32[]{:S(2)}, u32[]{:S(2)}) collective-permute-start(f32[8,128]{1,0:T(8,128)S(1)} %get-tuple-element.39.refs_8_), channel_id=1, source_target_pairs={{0,11},{1,10},{2,9},{3,8},{4,15},{5,14},{6,13},{7,12},{8,3},{9,2},... | collective-permute-start | bytes 12296 | tf_op jit(solution)/shard_map/ppermute | solution.py:46
  194.0 8.8 %collective-permute-start.69 = (f32[8,128]{1,0:T(8,128)S(1)}, f32[8,128]{1,0:T(8,128)S(1)}, u32[]{:S(2)}, u32[]{:S(2)}) collective-permute-start(f32[8,128]{1,0:T(8,128)S(1)} %get-tuple-element.39.refs_8_), channel_id=1, source_target_pairs={{0,10},{1,11},{2,8},{3,9},{4,14},{5,15},{6,12},{7,13},{8,2},{9,3},... | collective-permute-start | bytes 12296 | tf_op jit(solution)/shard_map/ppermute | solution.py:46
  197.4 7.2 %collective-permute-start.68 = (f32[8,128]{1,0:T(8,128)S(1)}, f32[8,128]{1,0:T(8,128)S(1)}, u32[]{:S(2)}, u32[]{:S(2)}) collective-permute-start(f32[8,128]{1,0:T(8,128)S(1)} %get-tuple-element.39.refs_8_), channel_id=1, source_target_pairs={{0,9},{1,8},{2,11},{3,10},{4,13},{5,12},{6,15},{7,14},{8,1},{9,0},... | collective-permute-start | bytes 12296 | tf_op jit(solution)/shard_map/ppermute | solution.py:46
  197.8 6.8 %collective-permute-start.67 = (f32[8,128]{1,0:T(8,128)S(1)}, f32[8,128]{1,0:T(8,128)S(1)}, u32[]{:S(2)}, u32[]{:S(2)}) collective-permute-start(f32[8,128]{1,0:T(8,128)S(1)} %get-tuple-element.39.refs_8_), channel_id=1, source_target_pairs={{0,8},{1,9},{2,10},{3,11},{4,12},{5,13},{6,14},{7,15},{8,0},{9,1},... | collective-permute-start | bytes 12296 | tf_op jit(solution)/shard_map/ppermute | solution.py:46
  202.5 13.9 %collective-permute-start.59 = (f32[32,128]{1,0:T(8,128)S(1)}, f32[32,128]{1,0:T(8,128)S(1)}, u32[]{:S(2)}, u32[]{:S(2)}) collective-permute-start(f32[32,128]{1,0:T(8,128)S(1)} %get-tuple-element.38.refs_4_), channel_id=1, source_target_pairs={{0,3},{1,2},{2,1},{3,0},{4,7},{5,6},{6,5},{7,4},{8,11},{9,10},{10,... | collective-permute-start | bytes 49160 | tf_op jit(solution)/shard_map/ppermute | solution.py:46
  202.8 13.6 %collective-permute-start.58 = (f32[32,128]{1,0:T(8,128)S(1)}, f32[32,128]{1,0:T(8,128)S(1)}, u32[]{:S(2)}, u32[]{:S(2)}) collective-permute-start(f32[32,128]{1,0:T(8,128)S(1)} %get-tuple-element.38.refs_4_), channel_id=1, source_target_pairs={{0,2},{1,3},{2,0},{3,1},{4,6},{5,7},{6,4},{7,5},{8,10},{9,11},{10,... | collective-permute-start | bytes 49160 | tf_op jit(solution)/shard_map/ppermute | solution.py:46
  204.6 11.8 %collective-permute-start.57 = (f32[32,128]{1,0:T(8,128)S(1)}, f32[32,128]{1,0:T(8,128)S(1)}, u32[]{:S(2)}, u32[]{:S(2)}) collective-permute-start(f32[32,128]{1,0:T(8,128)S(1)} %get-tuple-element.38.refs_4_), channel_id=1, source_target_pairs={{0,1},{1,0},{2,3},{3,2},{4,5},{5,4},{6,7},{7,6},{8,9},{9,8},{10,11... | collective-permute-start | bytes 49160 | tf_op jit(solution)/shard_map/ppermute | solution.py:46
  (31 other events, 113.5 us)
